TPU v7x, 32 devices: a whole 2x2x4 slice. The times are simulated.
32 devices in a mesh: panel: 2 (over y), row: 4 (over z), layer: 4 (over x, core).
Axes of the slice: x: 2, y: 2, z: 4, core: 2. Of those that a mesh axis runs over, the one named last changes fastest.
Arguments:
- layers: bfloat16 [4, 8192, 512], P('layer', 'row', 'panel'), parts along dimension 2, may hold values from -6 to 6
- table: bfloat16 [16, 128, 64], replicated, may hold values from -0.375 to 0.375
- fitting: bfloat16 [8192, 6600], P('row', 'layer'), may hold values from -0.09375 to 0.09375
- owner: int32 [4, 128, 1], P('layer', 'row'), may hold values from 0 to 3; in each aligned block of 32 rows (0 to 31, 32 to 63, ..., all dimensions but the last counted through in order) at most 16 rows name the same one
- local_slice: int32 [4, 128], P('layer', 'row'), may hold values from 0 to 15
- block_index: int32 [4, 128], P('layer', 'row'), may hold values from 0 to 31
- weight_index: int32 [4, 128], P('layer', 'row'), may hold values from 0 to 15
Outputs:
- actuators: bfloat16 [512, 6600], P(('panel', 'row'), 'layer'), parts along dimension 0
There are 2 independent parts, one for each index of `panel`. A program takes and returns all parts, laid end to end along the dimension named above; an argument that names none is the same for every part. Nothing has to cross between parts.
Inputs may be any that keep to these rules, and one draw needn't show every extreme that they name: `owner`: within the 32 entries of one layer on one row device (aligned blocks of 32 entries), no value is named more than 16 times, and in every draw some block names one value exactly 16 times.
All inputs are finite; a program needn't handle non-finite values.
Results may differ from a plain program's by a relative error of at most 0.0058.
Values may be sent and summed in bfloat16 or wider, within the bound.
No kernel may reach another device: no remote copies, remote signals or barrier semaphores. Data moves between devices by JAX's collectives and lax.ppermute only.
A program may use at most 64 MiB of HBM per device.

v0:
```python
import jax
import jax.numpy as jnp
from jax import lax
from jax.sharding import PartitionSpec as P


def local(layers, table, fitting, owner, local_slice, block_index, weight_index):
    rows_dev = layers.shape[1]
    columns = layers.shape[2]
    slice_rows = table.shape[1]
    block_rows = table.shape[2]
    entries = owner.shape[1]
    peer_count = lax.axis_size("row")
    capacity = max(2, 2 * entries // peer_count)
    slot_count = peer_count * capacity
    owned_slices = fitting.shape[0] // slice_rows
    owner_now = owner[0, :, 0]
    local_now = local_slice[0]
    owner_match = (owner_now[:, None] == jnp.arange(peer_count, dtype=jnp.int32)[None, :]).astype(
        jnp.int32
    )
    slot_rank = jnp.sum((jnp.cumsum(owner_match, axis=0) - 1) * owner_match, axis=1)
    target = owner_now * capacity + slot_rank
    placed = target[None, :] == jnp.arange(slot_count, dtype=jnp.int32)[:, None]
    filled = jnp.any(placed, axis=1)
    source = jnp.sum(jnp.where(placed, jnp.arange(entries, dtype=jnp.int32)[None, :], 0), axis=1)
    send_local = jnp.where(filled, local_now[source], -1).reshape(peer_count, capacity)
    grouped = layers[0].reshape(rows_dev // block_rows, block_rows, columns)
    picked = grouped[block_index[0][source]].reshape(peer_count, capacity, block_rows, columns)
    send_weight = weight_index[0][source].reshape(peer_count, capacity)
    got_rows, got_weight, got_local = (
        lax.all_to_all(picked, "row", split_axis=0, concat_axis=0, tiled=True),
        lax.all_to_all(send_weight, "row", split_axis=0, concat_axis=0, tiled=True),
        lax.all_to_all(send_local, "row", split_axis=0, concat_axis=0, tiled=True),
    )
    pupil_terms = jnp.einsum(
        "ksb,kbc->ksc",
        table[got_weight.reshape(-1)],
        got_rows.reshape(slot_count, block_rows, columns),
        preferred_element_type=jnp.float32,
    ).astype(jnp.bfloat16)
    selector = (
        jnp.arange(owned_slices, dtype=jnp.int32)[:, None] == got_local.reshape(-1)[None, :]
    ).astype(jnp.bfloat16)
    partial_pupil = jnp.dot(
        selector,
        pupil_terms.reshape(slot_count, slice_rows * columns),
        preferred_element_type=jnp.float32,
    ).reshape(owned_slices * slice_rows, columns)
    pupil_rounded = lax.psum(partial_pupil, "layer").astype(jnp.bfloat16)
    return lax.psum_scatter(
        lax.dot_general(
            pupil_rounded, fitting, (((0,), (0,)), ((), ())), preferred_element_type=jnp.float32
        ),
        "row",
        scatter_dimension=0,
        tiled=True,
    ).astype(jnp.bfloat16)


def solution(mesh):
    return jax.shard_map(
        local,
        mesh=mesh,
        in_specs=(
            P("layer", "row", "panel"),
            P(),
            P("row", "layer"),
            P("layer", "row", None),
            P("layer", "row"),
            P("layer", "row"),
            P("layer", "row"),
        ),
        out_specs=P(("panel", "row"), "layer"),
        check_vma=False,
    )
```

profile of v0, /device:TPU:0, one launch (start us, length us, event | category | flops | bytes accessed | tf_op | source)
XLA Modules:
  0.0 183.2 jit_solution(12246338649943333909)
XLA Ops:
  6.5 0.8 fusion.3
  7.4 0.8 select_reduce_fusion.1
  8.2 0.7 multiply_add_fusion
  9.0 1.4 gather_fusion.1
  10.4 0.7 all_to_all.14
  11.1 6.3 %all-to-all-start.1 = ((s32[4,1,16]{2,1,0:T(1,128)}), s32[4,1,16]{2,1,0:T(1,128)S(1)}, u32[]{:S(2)}, u32[]{:S(2)}) async-start(s32[4,1,16]{2,1,0:T(1,128)} %bitcast.6), calls=%async_computation.1 | async-start | bytes 4096 | tf_op jit(solution)/shard_map/all_to_all | solution.py:33
  17.5 1.4 gather_fusion.3
  19.0 1.4 gather_fusion
  20.4 0.7 select_n.54
  21.1 1.8 all-to-all-done.1
  22.9 3.3 %all-to-all-start = ((s32[4,1,16]{2,1,0:T(1,128)}), s32[4,1,16]{2,1,0:T(1,128)S(1)}, u32[]{:S(2)}, u32[]{:S(2)}) async-start(s32[4,1,16]{2,1,0:T(1,128)} %bitcast.4), calls=%async_computation | async-start | bytes 4096 | tf_op jit(solution)/shard_map/all_to_all | solution.py:34
  26.2 2.0 %gather_fusion.4 = bf16[64,64,256]{2,1,0:T(8,128)(2,1)} fusion(bf16[32,64,256]{2,1,0:T(8,128)(2,1)S(1)} %bitcast.27, s32[1024]{0:T(1024)S(1)} %pad_clamp_fusion), kind=kCustom, calls=%fused_computation.4 | custom fusion | bytes 4194560 | tf_op jit(solution)/shard_map/gather | solution.py:29
  28.2 3.5 %all-to-all-done = s32[4,1,16]{2,1,0:T(1,128)S(1)} async-done(((s32[4,1,16]{2,1,0:T(1,128)}), s32[4,1,16]{2,1,0:T(1,128)S(1)}, u32[]{:S(2)}, u32[]{:S(2)}) %all-to-all-start) | async-done | bytes 288 | tf_op jit(solution)/shard_map/all_to_all | solution.py:34
  31.7 4.6 %all-to-all-start.2 = ((bf16[4,16,64,256]{3,2,1,0:T(8,128)(2,1)}), bf16[4,16,64,256]{3,2,1,0:T(8,128)(2,1)}, u32[]{:S(2)}, u32[]{:S(2)}) async-start(bf16[4,16,64,256]{3,2,1,0:T(8,128)(2,1)} %bitcast.12), calls=%async_computation.2 | async-start | bytes 4194304 | tf_op jit(solution)/shard_map/all_to_all | solution.py:32
  37.6 0.7 reduce.7
  38.4 0.7 gather_fusion.2
  39.2 43.5 %all-to-all-done.2 = bf16[4,16,64,256]{3,2,1,0:T(8,128)(2,1)} async-done(((bf16[4,16,64,256]{3,2,1,0:T(8,128)(2,1)}), bf16[4,16,64,256]{3,2,1,0:T(8,128)(2,1)}, u32[]{:S(2)}, u32[]{:S(2)}) %all-to-all-start.2) | async-done | bytes 2097184 | tf_op jit(solution)/shard_map/all_to_all | solution.py:32
  82.7 2.9 %convolution_convert_fusion = bf16[64,128,256]{2,1,0:T(8,128)(2,1)S(1)} fusion(bf16[64,128,64]{1,2,0:T(8,128)(2,1)S(1)} %gather_fusion.2, bf16[64,64,256]{2,1,0:T(8,128)(2,1)} %bitcast.13), kind=kOutput, calls=%fused_computation.5 | convolution fusion | flops 270532608 | bytes 7340032 | tf_op jit(solution)/shard_map/ksb,kbc->ksc/dot_general | solution.py:36
  85.6 2.6 %copy.12 = bf16[8,8,128,256]{3,1,2,0:T(8,128)(2,1)S(1)} copy(bf16[8,8,128,256]{3,2,1,0:T(8,128)(2,1)S(1)} %bitcast.31) | data formatting | bytes 8388608
  88.9 1.5 reshape.113
  90.4 40.8 %all-reduce.1 = bf16[2048,256]{1,0:T(8,128)(2,1)S(1)} all-reduce(f32[2048,256]{1,0:T(8,128)} %reshape.113), channel_id=1, replica_groups=mesh['panel'=2,'row'=4,'layer'=4] {'layer'}, use_global_device_ids=true, to_apply=%region_4.5 | all-reduce | flops 524288 | bytes 3145728 | tf_op jit(solution)/shard_map/psum | solution.py:50
  131.2 6.2 %fusion.9 = f32[256,1650]{1,0:T(8,128)} fusion(bf16[2048,256]{1,0:T(8,128)(2,1)S(1)} %all-reduce.1, bf16[2048,1650]{0,1:T(8,128)(2,1)} %param.9), kind=kOutput, calls=%fused_computation.28 | convolution fusion | flops 1730150400 | bytes 9496576 | tf_op jit(solution)/shard_map/dot_general | solution.py:52
  137.5 37.1 %reduce-scatter.2.cloned.1.call-done = f32[64,1650]{1,0:T(8,128)} async-done(((f32[256,1650]{1,0:T(8,128)}), f32[64,1650]{1,0:T(8,128)}) %reduce-scatter.2.cloned.1.call-update) | async-done | bytes 422416 | tf_op jit(solution)/shard_map/reduce_scatter | solution.py:51
  174.6 1.7 convert_element_type.16
  (21 shorter events, 2.4 us)
Async XLA Ops:
  6.5 19.7 %copy-start = (bf16[1,2048,256]{2,1,0:T(8,128)(2,1)S(1)}, bf16[1,2048,256]{2,1,0:T(8,128)(2,1)}, u32[]{:S(2)}) copy-start(bf16[1,2048,256]{2,1,0:T(8,128)(2,1)} %param.7) | copy-start | bytes 3145732
  11.1 11.8 %all-to-all-start.1 = ((s32[4,1,16]{2,1,0:T(1,128)}), s32[4,1,16]{2,1,0:T(1,128)S(1)}, u32[]{:S(2)}, u32[]{:S(2)}) async-start(s32[4,1,16]{2,1,0:T(1,128)} %bitcast.6), calls=%async_computation.1 | async-start | bytes 4096 | tf_op jit(solution)/shard_map/all_to_all | solution.py:33
  22.9 8.8 %all-to-all-start = ((s32[4,1,16]{2,1,0:T(1,128)}), s32[4,1,16]{2,1,0:T(1,128)S(1)}, u32[]{:S(2)}, u32[]{:S(2)}) async-start(s32[4,1,16]{2,1,0:T(1,128)} %bitcast.4), calls=%async_computation | async-start | bytes 4096 | tf_op jit(solution)/shard_map/all_to_all | solution.py:34
  31.7 6.7 %copy-start.1 = (bf16[16,128,64]{1,2,0:T(8,128)(2,1)S(1)}, bf16[16,128,64]{1,2,0:T(8,128)(2,1)}, u32[]{:S(2)}) copy-start(bf16[16,128,64]{1,2,0:T(8,128)(2,1)} %param.8) | copy-start | bytes 786436
  31.7 51.0 %all-to-all-start.2 = ((bf16[4,16,64,256]{3,2,1,0:T(8,128)(2,1)}), bf16[4,16,64,256]{3,2,1,0:T(8,128)(2,1)}, u32[]{:S(2)}, u32[]{:S(2)}) async-start(bf16[4,16,64,256]{3,2,1,0:T(8,128)(2,1)} %bitcast.12), calls=%async_computation.2 | async-start | bytes 4194304 | tf_op jit(solution)/shard_map/all_to_all | solution.py:32
  36.3 138.3 %reduce-scatter.2.cloned.1.call-start = ((), (), s32[]{:S(2)}) async-start(), calls=%async_computation.4 | async-start | bytes 2129920 | tf_op jit(solution)/shard_map/reduce_scatter | solution.py:51
Sparse Core Ops, SparseCore 0:
  137.6 36.9 reduce-scatter.1
where the time goes:
time: 184 us; the launch traced here: 183 us
  waiting for transfers between devices  86 us (47%)
  blocking collectives  40.8 us (22%)
  starting transfers between devices  14.2 us (8%)
  between operations  13.5 us (7%)
  local copies, waits for them, and re-layouts  13.2 us (7%)
  matrix products  9.8 us (5%)
  other arithmetic  5.64 us (3%)
    all_to_all x1, waiting for transfers between devices, local(): lax.all_to_all(picked, 'row', split_axis=0, concat_axis=0, tiled=True)  43.5 us
    psum x1, blocking collectives, local(): pupil_rounded = lax.psum(partial_pupil, 'layer').astype(jnp.bfloat16)  40.8 us
    reduce_scatter x1, waiting for transfers between devices, local(): lax.psum_scatter(lax.dot_general(pupil_rounded, fitting, (((0,), (0,)), (...  37.1 us
    all_to_all x1, starting transfers between devices, local(): lax.all_to_all(send_weight, 'row', split_axis=0, concat_axis=0, tiled=True)  6.32 us
    dot_general x1, matrix products, local(): lax.dot_general(pupil_rounded, fitting, (((0,), (0,)), ((), ())), preferr...  6.24 us
    all_to_all x1, starting transfers between devices, local(): lax.all_to_all(picked, 'row', split_axis=0, concat_axis=0, tiled=True)  4.58 us
  transfers between devices with their start and end apart: 4, of which 4 were waited for; matrix products, arithmetic and copies ran while one was open for 5% of the time, Pallas kernels for 0%

commit v1 on v0

v1 whole, which is shorter than its diff:
```python
import functools

import jax
import jax.numpy as jnp
from jax import lax
from jax.experimental import pallas as pl
from jax.experimental.pallas import tpu as pltpu
from jax.sharding import PartitionSpec as P

LANES = 128
F32, BF16 = jnp.float32, jnp.bfloat16
VMEM = pl.BlockSpec(memory_space=pltpu.VMEM)
SMEM = pl.BlockSpec(memory_space=pltpu.SMEM)
PARAMS = dict(vmem_limit_bytes=48 * 1024 * 1024)


def turn_kernel(layers_ref, *outs):
    columns = layers_ref.shape[1]
    each = outs[0].shape[0]
    first = lax.axis_index("layer") * each
    row = lax.broadcasted_iota(jnp.int32, (columns, columns), 0)
    col = lax.broadcasted_iota(jnp.int32, (columns, columns), 1)
    pick = (col == lax.rem(row + first, columns)).astype(BF16)
    turned = lax.dot_general(
        pick, layers_ref[...], (((1,), (1,)), ((), ())), preferred_element_type=F32
    ).astype(BF16)
    for k, out in enumerate(outs):
        out[...] = turned[k * each : (k + 1) * each]


def pupil_kernel(n_layer, n_row, unroll, table_ref, *refs):
    codes, parts = refs[:n_layer], refs[n_layer : 2 * n_layer]
    outs, total = refs[2 * n_layer : 2 * n_layer + n_row], refs[-1]
    weights = table_ref.shape[0] // 2
    owned = outs[0].shape[1] // LANES
    total[...] = jnp.zeros_like(total)
    for code, part in zip(codes, parts):

        def step(group, carry):
            terms = []
            for u in range(unroll):
                e = group * unroll + u
                block = code[1, e]
                source = part[:, pl.ds(pl.multiple_of((block // 2) * LANES, LANES), LANES)]
                weight = table_ref[lax.rem(block, 2) * weights + code[2, e]]
                terms.append((code[0, e], jnp.dot(source, weight, preferred_element_type=F32)))
            for dest, term in terms:
                total[dest] += term
            return carry

        lax.fori_loop(0, code.shape[1] // unroll, step, 0)
    me = lax.axis_index("row")
    for k, out in enumerate(outs):
        base = lax.rem(me + k, n_row) * owned
        for s in range(owned):
            out[:, s * LANES : (s + 1) * LANES] = total[base + s].astype(BF16)


def fit_kernel(n_layer, n_row, fitting_ref, *refs):
    pieces, outs = refs[:n_layer], refs[n_layer : n_layer + n_row]
    left, product = refs[-2], refs[-1]

    @pl.when(pl.program_id(0) == 0)
    def _():
        me = lax.axis_index("layer")
        for j, piece in enumerate(pieces):
            left[lax.rem(me + n_layer - j, n_layer)] = piece[...]

    columns = product.shape[0]
    product[...] = jnp.dot(
        left[...].reshape(columns, left.shape[2]), fitting_ref[...], preferred_element_type=F32
    )
    each = columns // n_row
    me = lax.axis_index("row")
    for k, out in enumerate(outs):
        start = pl.multiple_of(lax.rem(me + k, n_row) * each, each)
        out[...] = product[pl.ds(start, each), :].astype(BF16)


def exchange(chunks, axis):
    n = len(chunks)
    return [
        chunk if k == 0 else lax.ppermute(chunk, axis, [(i, (i + k) % n) for i in range(n)])
        for k, chunk in enumerate(chunks)
    ]


def total_of(parts):
    return sum(part.astype(F32) for part in parts).astype(BF16)


def local(layers, table, fitting, owner, local_slice, block_index, weight_index):
    n_layer, n_row = lax.axis_size("layer"), lax.axis_size("row")
    rows_dev, columns = layers.shape[1:]
    weights, slice_rows, block_rows = table.shape
    points, actuators = fitting.shape
    owned = points // slice_rows
    each = columns // n_layer

    dest = owner[0, :, 0] * owned + local_slice[0]
    code = jnp.stack([dest, block_index[0], weight_index[0]])
    codes = exchange([code] * n_layer, "layer")

    turned = pl.pallas_call(
        turn_kernel,
        out_shape=[jax.ShapeDtypeStruct((each, rows_dev), BF16)] * n_layer,
        in_specs=[VMEM],
        out_specs=[VMEM] * n_layer,
        compiler_params=pltpu.CompilerParams(**PARAMS),
    )(layers[0])
    parts = exchange(turned, "layer")

    flipped = jnp.swapaxes(table, 1, 2)
    nothing = jnp.zeros_like(flipped)
    padded = jnp.concatenate(
        [jnp.concatenate([flipped, nothing], 1), jnp.concatenate([nothing, flipped], 1)], 0
    )
    shares = pl.pallas_call(
        functools.partial(pupil_kernel, n_layer, n_row, 8),
        out_shape=[jax.ShapeDtypeStruct((each, points), BF16)] * n_row,
        in_specs=[VMEM] + [SMEM] * n_layer + [VMEM] * n_layer,
        out_specs=[VMEM] * n_row,
        scratch_shapes=[pltpu.VMEM((n_row * owned, each, slice_rows), F32)],
        compiler_params=pltpu.CompilerParams(**PARAMS),
    )(padded, *codes, *parts)
    pupil = total_of(exchange(shares, "row"))
    pieces = exchange([pupil] * n_layer, "layer")

    tile = 2 * LANES
    partial = pl.pallas_call(
        functools.partial(fit_kernel, n_layer, n_row),
        grid=(pl.cdiv(actuators, tile),),
        out_shape=[jax.ShapeDtypeStruct((columns // n_row, actuators), BF16)] * n_row,
        in_specs=[pl.BlockSpec((points, tile), lambda i: (0, i))] + [VMEM] * n_layer,
        out_specs=[pl.BlockSpec((columns // n_row, tile), lambda i: (0, i))] * n_row,
        scratch_shapes=[
            pltpu.VMEM((n_layer, each, points), BF16),
            pltpu.VMEM((columns, tile), F32),
        ],
        compiler_params=pltpu.CompilerParams(**PARAMS),
    )(fitting, *pieces)
    return total_of(exchange(partial, "row"))


def solution(mesh):
    return jax.shard_map(
        local,
        mesh=mesh,
        in_specs=(
            P("layer", "row", "panel"),
            P(),
            P("row", "layer"),
            P("layer", "row", None),
            P("layer", "row"),
            P("layer", "row"),
            P("layer", "row"),
        ),
        out_specs=P(("panel", "row"), "layer"),
        check_vma=False,
    )
```

time: 184 us -> 89.7 us (0.49)
  the two profiles are of different devices: /device:TPU:0 before, /device:TPU:11 now
where the time goes in v1:
time: 89.7 us; the launch traced here: 89.2 us
  waiting for transfers between devices  49.5 us (55%)
  starting transfers between devices  13.1 us (15%)
  Pallas kernels  12.1 us (13%)
  local copies, waits for them, and re-layouts  10.9 us (12%)
  other arithmetic  3.47 us (4%)
    ppermute x15, waiting for transfers between devices, exchange(): lax.ppermute(chunk, axis, [(i, (i + k) % n) for i in range(n)])  49.5 us
    ppermute x15, starting transfers between devices, exchange(): lax.ppermute(chunk, axis, [(i, (i + k) % n) for i in range(n)])  13.1 us
    unnamed x3, local copies, waits for them, and re-layouts  10.9 us
    pallas_call x1, Pallas kernels, local(): pl.pallas_call(functools.partial(fit_kernel, n_layer, n_row), grid=(pl.cd...  7.21 us
    pallas_call x1, Pallas kernels, local(): pl.pallas_call(functools.partial(pupil_kernel, n_layer, n_row, 8), out_sh...  4.39 us
  transfers between devices with their start and end apart: 15, of which 8 were waited for; matrix products, arithmetic and copies ran while one was open for 14% of the time, Pallas kernels for 0%

profile of v1, /device:TPU:11, one launch (start us, length us, event | category | flops | bytes accessed | tf_op | source)
XLA Modules:
  0.0 89.2 jit_solution(5754136906617759787)
XLA Ops:
  0.0 1.2 %copy-done = bf16[1,2048,256]{2,1,0:T(8,128)(2,1)S(1)} copy-done((bf16[1,2048,256]{2,1,0:T(8,128)(2,1)S(1)}, bf16[1,2048,256]{2,1,0:T(8,128)(2,1)}, u32[]{:S(2)}) %copy-start) | copy-done | bytes 1048600
  1.7 0.9 collective-permute-start.3
  2.6 1.2 %collective-permute-start.4 = (bf16[64,2048]{1,0:T(8,128)(2,1)S(1)}, bf16[64,2048]{1,0:T(8,128)(2,1)S(1)}, u32[]{:S(2)}, u32[]{:S(2)}) collective-permute-start(bf16[64,2048]{1,0:T(8,128)(2,1)S(1)} %get-tuple-element.19), channel_id=1, source_target_pairs={{0,2},{1,3},{2,0},{3,1},{4,6},{5,7},{6,4},{7,5},{8,10},{9,11},{10,... | collective-permute-start | bytes 786440 | tf_op jit(solution)/shard_map/ppermute | solution.py:83
  4.5 0.7 pad_add_fusion.refs_0_
  5.1 0.7 collective-permute-start.2
  5.8 1.2 %collective-permute-start.1 = (s32[3,32]{1,0:T(4,128)S(1)}, s32[3,32]{1,0:T(4,128)S(1)}, u32[]{:S(2)}, u32[]{:S(2)}) collective-permute-start(s32[3,32]{1,0:T(4,128)S(1)} %pad_add_fusion.refs_0_), channel_id=1, source_target_pairs={{0,2},{1,3},{2,0},{3,1},{4,6},{5,7},{6,4},{7,5},{8,10},{9,11},{10,... | collective-permute-start | bytes 1160 | tf_op jit(solution)/shard_map/ppermute | solution.py:83
  7.1 9.0 %collective-permute-done.2.refs_3_ = s32[3,32]{1,0:T(4,128)S(1)} collective-permute-done((s32[3,32]{1,0:T(4,128)S(1)}, s32[3,32]{1,0:T(4,128)S(1)}, u32[]{:S(2)}, u32[]{:S(2)}) %collective-permute-start.2) | collective-permute-done | bytes 416 | tf_op jit(solution)/shard_map/ppermute | solution.py:83
  16.0 1.2 %fusion.2.table_ref = bf16[32,128,128]{2,1,0:T(8,128)(2,1)S(1)} fusion(bf16[16,64,128]{2,1,0:T(8,128)(2,1)} %bitcast.5), kind=kLoop, calls=%fused_computation.4 | loop fusion | flops 4194304 | bytes 1310720 | tf_op jit(solution)/shard_map/concatenate | solution.py:115
  17.3 4.4 %shard_map.74 = (bf16[64,2048]{1,0:T(8,128)(2,1)S(1)}, bf16[64,2048]{1,0:T(8,128)(2,1)S(1)}, bf16[64,2048]{1,0:T(8,128)(2,1)S(1)}, bf16[64,2048]{1,0:T(8,128)(2,1)S(1)}) custom-call(bf16[32,128,128]{2,1,0:T(8,128)(2,1)S(1)} %fusion.2.table_ref, s32[3,32]{1,0:T(4,128)S(1)} %pad_add_fusion.refs_0_, s32[3,32]{1,0:T(4,128)S(1)} %collective-permute-done.refs_1_, ...), custom_call_target="tpu_custom_call" | custom-call | tf_op jit(solution)/shard_map/pallas_call | solution.py:118
  21.7 1.4 %collective-permute-start.6 = (bf16[64,2048]{1,0:T(8,128)(2,1)S(1)}, bf16[64,2048]{1,0:T(8,128)(2,1)S(1)}, u32[]{:S(2)}, u32[]{:S(2)}) collective-permute-start(bf16[64,2048]{1,0:T(8,128)(2,1)S(1)} %get-tuple-element.22), channel_id=1, source_target_pairs={{0,4},{4,8},{8,12},{12,0},{1,5},{5,9},{9,13},{13,1},{2,6},{6,10},{... | collective-permute-start | bytes 786440 | tf_op jit(solution)/shard_map/ppermute | solution.py:83
  23.0 1.1 %collective-permute-start.7 = (bf16[64,2048]{1,0:T(8,128)(2,1)S(1)}, bf16[64,2048]{1,0:T(8,128)(2,1)S(1)}, u32[]{:S(2)}, u32[]{:S(2)}) collective-permute-start(bf16[64,2048]{1,0:T(8,128)(2,1)S(1)} %get-tuple-element.23), channel_id=1, source_target_pairs={{0,8},{4,12},{8,0},{12,4},{1,9},{5,13},{9,1},{13,5},{2,10},{6,14},... | collective-permute-start | bytes 786440 | tf_op jit(solution)/shard_map/ppermute | solution.py:83
  24.1 1.4 %collective-permute-start.8 = (bf16[64,2048]{1,0:T(8,128)(2,1)S(1)}, bf16[64,2048]{1,0:T(8,128)(2,1)S(1)}, u32[]{:S(2)}, u32[]{:S(2)}) collective-permute-start(bf16[64,2048]{1,0:T(8,128)(2,1)S(1)} %get-tuple-element.24), channel_id=1, source_target_pairs={{0,12},{4,0},{8,4},{12,8},{1,13},{5,1},{9,5},{13,9},{2,14},{6,2},{... | collective-permute-start | bytes 786440 | tf_op jit(solution)/shard_map/ppermute | solution.py:83
  25.5 3.4 %collective-permute-done.6 = bf16[64,2048]{1,0:T(8,128)(2,1)S(1)} collective-permute-done((bf16[64,2048]{1,0:T(8,128)(2,1)S(1)}, bf16[64,2048]{1,0:T(8,128)(2,1)S(1)}, u32[]{:S(2)}, u32[]{:S(2)}) %collective-permute-start.6) | collective-permute-done | bytes 262176 | tf_op jit(solution)/shard_map/ppermute | solution.py:83
  28.9 15.9 %collective-permute-done.7 = bf16[64,2048]{1,0:T(8,128)(2,1)S(1)} collective-permute-done((bf16[64,2048]{1,0:T(8,128)(2,1)S(1)}, bf16[64,2048]{1,0:T(8,128)(2,1)S(1)}, u32[]{:S(2)}, u32[]{:S(2)}) %collective-permute-start.7) | collective-permute-done | bytes 262176 | tf_op jit(solution)/shard_map/ppermute | solution.py:83
  44.8 2.9 %collective-permute-done.8 = bf16[64,2048]{1,0:T(8,128)(2,1)S(1)} collective-permute-done((bf16[64,2048]{1,0:T(8,128)(2,1)S(1)}, bf16[64,2048]{1,0:T(8,128)(2,1)S(1)}, u32[]{:S(2)}, u32[]{:S(2)}) %collective-permute-start.8) | collective-permute-done | bytes 262176 | tf_op jit(solution)/shard_map/ppermute | solution.py:83
  48.6 1.5 %collective-permute-start.9 = (bf16[64,2048]{1,0:T(8,128)(2,1)S(1)}, bf16[64,2048]{1,0:T(8,128)(2,1)S(1)}, u32[]{:S(2)}, u32[]{:S(2)}) collective-permute-start(bf16[64,2048]{1,0:T(8,128)(2,1)S(1)} %add_convert_fusion.refs_0_), channel_id=1, source_target_pairs={{0,1},{1,2},{2,3},{3,0},{4,5},{5,6},{6,7},{7,4},{8,9},{9,10},{10,1... | collective-permute-start | bytes 786440 | tf_op jit(solution)/shard_map/ppermute | solution.py:83
  50.2 9.7 %copy.8.fitting_ref = bf16[2048,1650]{1,0:T(8,128)(2,1)} copy(bf16[2048,1650]{0,1:T(8,128)(2,1)} %param.9) | data formatting | bytes 13516800 | tf_op args[2]
  60.3 7.2 %shard_map.75 = (bf16[64,1650]{1,0:T(8,128)(2,1)S(1)}, bf16[64,1650]{1,0:T(8,128)(2,1)S(1)}, bf16[64,1650]{1,0:T(8,128)(2,1)S(1)}, bf16[64,1650]{1,0:T(8,128)(2,1)S(1)}) custom-call(bf16[2048,1650]{1,0:T(8,128)(2,1)} %copy.8.fitting_ref, bf16[64,2048]{1,0:T(8,128)(2,1)S(1)} %add_convert_fusion.refs_0_, bf16[64,2048]{1,0:T(8,128)(2,1)S(1)} %collective-permute-done.9.refs_1_, ...), custom_call_target="tpu_custom_call" | custom-call | tf_op jit(solution)/shard_map/pallas_call | solution.py:130
  67.6 1.5 %collective-permute-start.13 = (bf16[64,1650]{1,0:T(8,128)(2,1)S(1)}, bf16[64,1650]{1,0:T(8,128)(2,1)S(1)}, u32[]{:S(2)}, u32[]{:S(2)}) collective-permute-start(bf16[64,1650]{1,0:T(8,128)(2,1)S(1)} %get-tuple-element.27), channel_id=1, source_target_pairs={{0,8},{4,12},{8,0},{12,4},{1,9},{5,13},{9,1},{13,5},{2,10},{6,14},... | collective-permute-start | bytes 633608 | tf_op jit(solution)/shard_map/ppermute | solution.py:83
  69.0 1.4 %collective-permute-start.14 = (bf16[64,1650]{1,0:T(8,128)(2,1)S(1)}, bf16[64,1650]{1,0:T(8,128)(2,1)S(1)}, u32[]{:S(2)}, u32[]{:S(2)}) collective-permute-start(bf16[64,1650]{1,0:T(8,128)(2,1)S(1)} %get-tuple-element.28), channel_id=1, source_target_pairs={{0,12},{4,0},{8,4},{12,8},{1,13},{5,1},{9,5},{13,9},{2,14},{6,2},{... | collective-permute-start | bytes 633608 | tf_op jit(solution)/shard_map/ppermute | solution.py:83
  70.4 1.8 %collective-permute-done.12 = bf16[64,1650]{1,0:T(8,128)(2,1)S(1)} collective-permute-done((bf16[64,1650]{1,0:T(8,128)(2,1)S(1)}, bf16[64,1650]{1,0:T(8,128)(2,1)S(1)}, u32[]{:S(2)}, u32[]{:S(2)}) %collective-permute-start.12) | collective-permute-done | bytes 211232 | tf_op jit(solution)/shard_map/ppermute | solution.py:83
  72.2 11.3 %collective-permute-done.13 = bf16[64,1650]{1,0:T(8,128)(2,1)S(1)} collective-permute-done((bf16[64,1650]{1,0:T(8,128)(2,1)S(1)}, bf16[64,1650]{1,0:T(8,128)(2,1)S(1)}, u32[]{:S(2)}, u32[]{:S(2)}) %collective-permute-start.13) | collective-permute-done | bytes 211232 | tf_op jit(solution)/shard_map/ppermute | solution.py:83
  83.5 4.9 %collective-permute-done.14 = bf16[64,1650]{1,0:T(8,128)(2,1)S(1)} collective-permute-done((bf16[64,1650]{1,0:T(8,128)(2,1)S(1)}, bf16[64,1650]{1,0:T(8,128)(2,1)S(1)}, u32[]{:S(2)}, u32[]{:S(2)}) %collective-permute-start.14) | collective-permute-done | bytes 211232 | tf_op jit(solution)/shard_map/ppermute | solution.py:83
  88.4 0.8 add_convert_fusion.1
  (17 shorter events, 2.5 us)
Async XLA Ops:
  0.0 1.2 %copy-start = (bf16[1,2048,256]{2,1,0:T(8,128)(2,1)S(1)}, bf16[1,2048,256]{2,1,0:T(8,128)(2,1)}, u32[]{:S(2)}) copy-start(bf16[1,2048,256]{2,1,0:T(8,128)(2,1)} %param.7) | copy-start | bytes 3145732
  1.7 15.5 %collective-permute-start.3 = (bf16[64,2048]{1,0:T(8,128)(2,1)S(1)}, bf16[64,2048]{1,0:T(8,128)(2,1)S(1)}, u32[]{:S(2)}, u32[]{:S(2)}) collective-permute-start(bf16[64,2048]{1,0:T(8,128)(2,1)S(1)} %get-tuple-element.18), channel_id=1, source_target_pairs={{0,1},{1,2},{2,3},{3,0},{4,5},{5,6},{6,7},{7,4},{8,9},{9,10},{10,1... | collective-permute-start | bytes 786440 | tf_op jit(solution)/shard_map/ppermute | solution.py:83
  2.6 14.7 %collective-permute-start.4 = (bf16[64,2048]{1,0:T(8,128)(2,1)S(1)}, bf16[64,2048]{1,0:T(8,128)(2,1)S(1)}, u32[]{:S(2)}, u32[]{:S(2)}) collective-permute-start(bf16[64,2048]{1,0:T(8,128)(2,1)S(1)} %get-tuple-element.19), channel_id=1, source_target_pairs={{0,2},{1,3},{2,0},{3,1},{4,6},{5,7},{6,4},{7,5},{8,10},{9,11},{10,... | collective-permute-start | bytes 786440 | tf_op jit(solution)/shard_map/ppermute | solution.py:83
  3.8 13.5 %collective-permute-start.5 = (bf16[64,2048]{1,0:T(8,128)(2,1)S(1)}, bf16[64,2048]{1,0:T(8,128)(2,1)S(1)}, u32[]{:S(2)}, u32[]{:S(2)}) collective-permute-start(bf16[64,2048]{1,0:T(8,128)(2,1)S(1)} %get-tuple-element.20), channel_id=1, source_target_pairs={{0,3},{1,0},{2,1},{3,2},{4,7},{5,4},{6,5},{7,6},{8,11},{9,8},{10,9... | collective-permute-start | bytes 786440 | tf_op jit(solution)/shard_map/ppermute | solution.py:83
  5.1 10.9 %collective-permute-start.2 = (s32[3,32]{1,0:T(4,128)S(1)}, s32[3,32]{1,0:T(4,128)S(1)}, u32[]{:S(2)}, u32[]{:S(2)}) collective-permute-start(s32[3,32]{1,0:T(4,128)S(1)} %pad_add_fusion.refs_0_), channel_id=1, source_target_pairs={{0,3},{1,0},{2,1},{3,2},{4,7},{5,4},{6,5},{7,6},{8,11},{9,8},{10,9... | collective-permute-start | bytes 1160 | tf_op jit(solution)/shard_map/ppermute | solution.py:83
  5.8 11.4 %collective-permute-start.1 = (s32[3,32]{1,0:T(4,128)S(1)}, s32[3,32]{1,0:T(4,128)S(1)}, u32[]{:S(2)}, u32[]{:S(2)}) collective-permute-start(s32[3,32]{1,0:T(4,128)S(1)} %pad_add_fusion.refs_0_), channel_id=1, source_target_pairs={{0,2},{1,3},{2,0},{3,1},{4,6},{5,7},{6,4},{7,5},{8,10},{9,11},{10,... | collective-permute-start | bytes 1160 | tf_op jit(solution)/shard_map/ppermute | solution.py:83
  16.0 1.2 %collective-permute-start = (s32[3,32]{1,0:T(4,128)S(1)}, s32[3,32]{1,0:T(4,128)S(1)}, u32[]{:S(2)}, u32[]{:S(2)}) collective-permute-start(s32[3,32]{1,0:T(4,128)S(1)} %pad_add_fusion.refs_0_), channel_id=1, source_target_pairs={{0,1},{1,2},{2,3},{3,0},{4,5},{5,6},{6,7},{7,4},{8,9},{9,10},{10,1... | collective-permute-start | bytes 1160 | tf_op jit(solution)/shard_map/ppermute | solution.py:83
  21.7 7.2 %collective-permute-start.6 = (bf16[64,2048]{1,0:T(8,128)(2,1)S(1)}, bf16[64,2048]{1,0:T(8,128)(2,1)S(1)}, u32[]{:S(2)}, u32[]{:S(2)}) collective-permute-start(bf16[64,2048]{1,0:T(8,128)(2,1)S(1)} %get-tuple-element.22), channel_id=1, source_target_pairs={{0,4},{4,8},{8,12},{12,0},{1,5},{5,9},{9,13},{13,1},{2,6},{6,10},{... | collective-permute-start | bytes 786440 | tf_op jit(solution)/shard_map/ppermute | solution.py:83
  23.0 21.8 %collective-permute-start.7 = (bf16[64,2048]{1,0:T(8,128)(2,1)S(1)}, bf16[64,2048]{1,0:T(8,128)(2,1)S(1)}, u32[]{:S(2)}, u32[]{:S(2)}) collective-permute-start(bf16[64,2048]{1,0:T(8,128)(2,1)S(1)} %get-tuple-element.23), channel_id=1, source_target_pairs={{0,8},{4,12},{8,0},{12,4},{1,9},{5,13},{9,1},{13,5},{2,10},{6,14},... | collective-permute-start | bytes 786440 | tf_op jit(solution)/shard_map/ppermute | solution.py:83
  24.1 23.6 %collective-permute-start.8 = (bf16[64,2048]{1,0:T(8,128)(2,1)S(1)}, bf16[64,2048]{1,0:T(8,128)(2,1)S(1)}, u32[]{:S(2)}, u32[]{:S(2)}) collective-permute-start(bf16[64,2048]{1,0:T(8,128)(2,1)S(1)} %get-tuple-element.24), channel_id=1, source_target_pairs={{0,12},{4,0},{8,4},{12,8},{1,13},{5,1},{9,5},{13,9},{2,14},{6,2},{... | collective-permute-start | bytes 786440 | tf_op jit(solution)/shard_map/ppermute | solution.py:83
  47.8 12.1 %collective-permute-start.11 = (bf16[64,2048]{1,0:T(8,128)(2,1)S(1)}, bf16[64,2048]{1,0:T(8,128)(2,1)S(1)}, u32[]{:S(2)}, u32[]{:S(2)}) collective-permute-start(bf16[64,2048]{1,0:T(8,128)(2,1)S(1)} %add_convert_fusion.refs_0_), channel_id=1, source_target_pairs={{0,3},{1,0},{2,1},{3,2},{4,7},{5,4},{6,5},{7,6},{8,11},{9,8},{10,9... | collective-permute-start | bytes 786440 | tf_op jit(solution)/shard_map/ppermute | solution.py:83
  48.4 11.5 %collective-permute-start.10 = (bf16[64,2048]{1,0:T(8,128)(2,1)S(1)}, bf16[64,2048]{1,0:T(8,128)(2,1)S(1)}, u32[]{:S(2)}, u32[]{:S(2)}) collective-permute-start(bf16[64,2048]{1,0:T(8,128)(2,1)S(1)} %add_convert_fusion.refs_0_), channel_id=1, source_target_pairs={{0,2},{1,3},{2,0},{3,1},{4,6},{5,7},{6,4},{7,5},{8,10},{9,11},{10,... | collective-permute-start | bytes 786440 | tf_op jit(solution)/shard_map/ppermute | solution.py:83
  48.6 11.7 %collective-permute-start.9 = (bf16[64,2048]{1,0:T(8,128)(2,1)S(1)}, bf16[64,2048]{1,0:T(8,128)(2,1)S(1)}, u32[]{:S(2)}, u32[]{:S(2)}) collective-permute-start(bf16[64,2048]{1,0:T(8,128)(2,1)S(1)} %add_convert_fusion.refs_0_), channel_id=1, source_target_pairs={{0,1},{1,2},{2,3},{3,0},{4,5},{5,6},{6,7},{7,4},{8,9},{9,10},{10,1... | collective-permute-start | bytes 786440 | tf_op jit(solution)/shard_map/ppermute | solution.py:83
  67.5 4.7 %collective-permute-start.12 = (bf16[64,1650]{1,0:T(8,128)(2,1)S(1)}, bf16[64,1650]{1,0:T(8,128)(2,1)S(1)}, u32[]{:S(2)}, u32[]{:S(2)}) collective-permute-start(bf16[64,1650]{1,0:T(8,128)(2,1)S(1)} %get-tuple-element.26), channel_id=1, source_target_pairs={{0,4},{4,8},{8,12},{12,0},{1,5},{5,9},{9,13},{13,1},{2,6},{6,10},{... | collective-permute-start | bytes 633608 | tf_op jit(solution)/shard_map/ppermute | solution.py:83
  67.6 15.9 %collective-permute-start.13 = (bf16[64,1650]{1,0:T(8,128)(2,1)S(1)}, bf16[64,1650]{1,0:T(8,128)(2,1)S(1)}, u32[]{:S(2)}, u32[]{:S(2)}) collective-permute-start(bf16[64,1650]{1,0:T(8,128)(2,1)S(1)} %get-tuple-element.27), channel_id=1, source_target_pairs={{0,8},{4,12},{8,0},{12,4},{1,9},{5,13},{9,1},{13,5},{2,10},{6,14},... | collective-permute-start | bytes 633608 | tf_op jit(solution)/shard_map/ppermute | solution.py:83
  69.0 19.3 %collective-permute-start.14 = (bf16[64,1650]{1,0:T(8,128)(2,1)S(1)}, bf16[64,1650]{1,0:T(8,128)(2,1)S(1)}, u32[]{:S(2)}, u32[]{:S(2)}) collective-permute-start(bf16[64,1650]{1,0:T(8,128)(2,1)S(1)} %get-tuple-element.28), channel_id=1, source_target_pairs={{0,12},{4,0},{8,4},{12,8},{1,13},{5,1},{9,5},{13,9},{2,14},{6,2},{... | collective-permute-start | bytes 633608 | tf_op jit(solution)/shard_map/ppermute | solution.py:83
